TPU v7x, 256 devices: a whole 4x4x8 slice. The times are simulated.
256 devices in a mesh: dp: 16 (over y, x), sx: 16 (over z, core).
Axes of the slice: x: 4, y: 4, z: 8, core: 2. Of those that a mesh axis runs over, the one named last changes fastest.
Arguments:
- hidden: bfloat16 [32768, 3200], P(('dp', 'sx')), parts along dimension 0, may hold values from -6 to 6
- norm_gain: bfloat16 [3200], replicated, may hold values from 0.5 to 1.5
- route_expert: int32 [32768, 1], P(('dp', 'sx')), parts along dimension 0, may hold values from 0 to 15, as said below
- route_weight: float32 [32768], P(('dp', 'sx')), parts along dimension 0, may hold values from 0.3 to 1
- priority: int32 [32768], P(('dp', 'sx')), parts along dimension 0, may hold values from 0 to 2047, each once
- expert_gate_up: bfloat16 [3200, 2, 10240], P(None, None, 'sx'), may hold values from -0.109375 to 0.109375
- expert_down: bfloat16 [10240, 3200], P('sx'), may hold values from -0.0625 to 0.0625
Outputs:
- layer_out: bfloat16 [32768, 3200], P(('dp', 'sx')), parts along dimension 0
There are 16 independent parts, one for each index of `dp`. A program takes and returns all parts, laid end to end along the dimension named above; an argument that names none is the same for every part. Nothing has to cross between parts.
Inputs may be any that keep to these rules, and one draw needn't show every extreme that they name: `route_expert`: in the rows of one device at most 64 tokens name expert 0, and in every draw some device's rows name it exactly 64 times.
All inputs are finite; a program needn't handle non-finite values.
Results may differ from a plain program's by a relative error of at most 0.007.
Values may be sent and summed in bfloat16 or wider, within the bound.
No kernel may reach another device: no remote copies, remote signals or barrier semaphores. Data moves between devices by JAX's collectives and lax.ppermute only.
A program may use at most 128 MiB of HBM per device.

v0:
```python
import jax
import jax.numpy as jnp
from jax import lax
from jax.sharding import PartitionSpec as P


def on_device(hidden, norm_gain, route_expert, route_weight, priority, expert_gate_up, expert_down):
    devices = lax.axis_size("sx")
    tok_dev = hidden.shape[0]
    slot_count = tok_dev // 2
    cap_rows = 3 * slot_count * devices // 8
    fr_dev = expert_down.shape[0]
    resid_float = hidden.astype(jnp.float32)
    scale_rows = lax.rsqrt(jnp.mean(resid_float * resid_float, axis=1, keepdims=True) + 1e-06)
    normed = (resid_float * scale_rows * norm_gain.astype(jnp.float32)[None, :]).astype(
        jnp.bfloat16
    )
    token_expert = route_expert[:, 0]
    flight_local = token_expert == 0
    table_expert, table_priority = (
        lax.all_gather(token_expert, "sx", axis=0, tiled=True),
        lax.all_gather(priority, "sx", axis=0, tiled=True),
    )
    table_flight = table_expert == 0
    rank_local = jnp.sum(
        (table_flight[None, :] & (table_priority[None, :] < priority[:, None])).astype(jnp.int32),
        axis=1,
    )
    kept_local = flight_local & (rank_local < cap_rows)
    local_index = jnp.arange(tok_dev, dtype=jnp.int32)
    before = (local_index[None, :] < local_index[:, None]) & flight_local[None, :]
    slot_local = jnp.sum(before.astype(jnp.int32), axis=1)
    selector = (
        (jnp.arange(slot_count, dtype=jnp.int32)[:, None] == slot_local[None, :])
        & kept_local[None, :]
    ).astype(jnp.bfloat16)
    packed = jnp.dot(selector, normed, preferred_element_type=jnp.float32).astype(jnp.bfloat16)
    gate_up_flat = expert_gate_up.reshape(expert_gate_up.shape[0], 2 * fr_dev)
    units_all = jnp.dot(
        lax.all_gather(packed, "sx", axis=0, tiled=True),
        gate_up_flat,
        preferred_element_type=jnp.float32,
    )
    activation_all = (jax.nn.silu(units_all[:, :fr_dev]) * units_all[:, fr_dev:]).astype(
        jnp.bfloat16
    )
    returned = lax.psum_scatter(
        jnp.dot(activation_all, expert_down, preferred_element_type=jnp.float32).astype(
            jnp.bfloat16
        ),
        "sx",
        scatter_dimension=0,
        tiled=True,
    )
    routed_slots = lax.optimization_barrier(returned).astype(jnp.float32)
    routed_local = jnp.take(routed_slots, jnp.clip(slot_local, 0, slot_count - 1), axis=0)
    routed_local = jnp.where(kept_local[:, None], routed_local, jnp.float32(0.0))
    total = resid_float + route_weight[:, None] * routed_local
    return total.astype(jnp.bfloat16)


def solution(mesh):
    in_specs = (
        P(("dp", "sx"), None),
        P(),
        P(("dp", "sx"), None),
        P(("dp", "sx")),
        P(("dp", "sx")),
        P(None, None, "sx"),
        P("sx", None),
    )
    out_specs = P(("dp", "sx"), None)
    return jax.shard_map(
        on_device, mesh=mesh, in_specs=in_specs, out_specs=out_specs, check_vma=False
    )
```

profile of v0, /device:TPU:1, one launch (start us, length us, event | category | flops | bytes accessed | tf_op | source)
XLA Modules:
  0.0 189.6 jit_solution(4170560351362747599)
XLA Ops:
  6.5 0.0 all-gather.4.cloned.1.call-start
  6.5 21.3 %all-gather = s32[2048,1]{0,1:T(1,128)S(1)} all-gather(s32[128,1]{0,1:T(1,128)} %param.9), channel_id=2, replica_groups=mesh['dp'=16,'sx'=16] {'sx'}, dimensions={0}, use_global_device_ids=true | all-gather | bytes 8704 | tf_op jit(solution)/shard_map/all_gather | solution.py:21
  27.9 14.5 %all-gather.1 = s32[16,1,128]{2,1,0:T(1,128)S(1)} all-gather(s32[1,1,128]{2,1,0:T(1,128)} %bitcast.24), channel_id=1, replica_groups=mesh['dp'=16,'sx'=16] {'sx'}, dimensions={0}, use_global_device_ids=true | all-gather | bytes 8704 | tf_op jit(solution)/shard_map/all_gather | solution.py:22
  42.4 0.9 convert_reduce_fusion
  43.3 0.7 fusion.15
  44.0 0.7 compare_and_fusion.1
  44.6 0.1 convert_reduce_fusion.1
  44.8 0.7 convert_element_type.34
  45.5 1.4 fusion.1
  46.9 2.3 %convolution_convert_fusion.1 = bf16[64,3200]{1,0:T(8,128)(2,1)} fusion(bf16[128,3200]{1,0:T(8,128)(2,1)} %param.7, f32[3200]{0:T(1024)S(1)} %convert_element_type.34, f32[128]{0:T(128)S(1)} %add_rsqrt_fusion, s32[128]{0:T(128)S(1)} %convert_reduce_fusion.1, pred[128]{0:T(512)(128)(4,1)S(1)} %compare_and_fusion.1), kind=kOutput, calls=%fused_computation.2 | convolution fusion | flops 54288384 | bytes 1242752 | tf_op jit(solution)/shard_map/dot_general | solution.py:37
  49.2 0.0 all-gather.4.cloned.1.call-update
  49.2 0.0 reduce-scatter.2.cloned.1.call-start
  49.3 7.9 %copy.8 = bf16[400,8,2,640]{3,1,2,0:T(8,128)(2,1)} copy(bf16[400,8,2,640]{3,2,1,0:T(2,128)(2,1)} %bitcast.21) | data formatting | bytes 16384000
  57.1 38.3 %all-gather.4.cloned.1.call-done = bf16[1024,3200]{1,0:T(8,128)(2,1)} async-done(((bf16[64,3200]{1,0:T(8,128)(2,1)}), bf16[1024,3200]{1,0:T(8,128)(2,1)}) %all-gather.4.cloned.1.call-update) | async-done | bytes 6553616 | tf_op jit(solution)/shard_map/all_gather | solution.py:40
  95.4 0.0 copy-start.2
  95.4 13.6 %fusion.18 = f32[1024,1280]{1,0:T(8,128)S(1)} fusion(bf16[1024,3200]{1,0:T(8,128)(2,1)} %all-gather.4.cloned.1.call-done, bf16[3200,1280]{1,0:T(8,128)(2,1)} %bitcast.22), kind=kOutput, calls=%fused_computation.35 | convolution fusion | flops 8388608000 | bytes 19988480 | tf_op jit(solution)/shard_map/dot_general | solution.py:39
  109.0 0.0 copy-done.2
  109.0 7.6 %convolution_convert_fusion = bf16[1024,3200]{1,0:T(8,128)(2,1)} fusion(bf16[640,3200]{1,0:T(8,128)(2,1)S(1)} %copy-done.2, f32[1024,1280]{1,0:T(8,128)S(1)} %fusion.18), kind=kOutput, calls=%fused_computation.1 | convolution fusion | flops 4201512960 | bytes 15892480 | tf_op jit(solution)/shard_map/dot_general | solution.py:48
  116.7 0.0 reduce-scatter.2.cloned.1.call-update
  116.7 62.3 %reduce-scatter.2.cloned.1.call-done = bf16[64,3200]{1,0:T(8,128)(2,1)} async-done(((bf16[1024,3200]{1,0:T(8,128)(2,1)}), bf16[64,3200]{1,0:T(8,128)(2,1)}) %reduce-scatter.2.cloned.1.call-update) | async-done | bytes 409616 | tf_op jit(solution)/shard_map/reduce_scatter | solution.py:47
  179.1 1.1 convert_element_type.39
  180.1 0.0 copy-start
  180.1 0.0 copy-start.1
  180.2 1.2 gather_fusion
  181.4 0.0 copy-done
  181.4 0.0 copy-done.1
  181.4 1.4 fusion.4
  (5 shorter events, 0.1 us)
Async XLA Ops:
  6.5 88.9 %all-gather.4.cloned.1.call-start = ((), (), s32[]{:S(2)}) async-start(), calls=%async_computation.1 | async-start | bytes 6963200 | tf_op jit(solution)/shard_map/all_gather | solution.py:40
  49.2 129.9 %reduce-scatter.2.cloned.1.call-start = ((), (), s32[]{:S(2)}) async-start(), calls=%async_computation.2 | async-start | bytes 6963200 | tf_op jit(solution)/shard_map/reduce_scatter | solution.py:47
  95.4 13.6 %copy-start.2 = (bf16[640,3200]{1,0:T(8,128)(2,1)S(1)}, bf16[640,3200]{1,0:T(8,128)(2,1)}, u32[]{:S(2)}) copy-start(bf16[640,3200]{1,0:T(8,128)(2,1)} %param.13) | copy-start | bytes 12288004
  180.1 1.3 copy-start
  180.1 1.3 copy-start.1
Sparse Core Ops, SparseCore 0:
  49.3 46.0 all-gather.3
  116.8 62.2 reduce-scatter.1
where the time goes:
time: 192 us; the launch traced here: 190 us
  waiting for transfers between devices  101 us (53%)
  blocking collectives  35.8 us (19%)
  matrix products  23.6 us (12%)
  between operations  13.5 us (7%)
  local copies, waits for them, and re-layouts  9.13 us (5%)
  other arithmetic  6.95 us (4%)
    reduce_scatter x1, waiting for transfers between devices, on_device(): lax.psum_scatter(jnp.dot(activation_all, expert_down, preferred_element_t...  62.3 us
    all_gather x1, waiting for transfers between devices, on_device(): lax.all_gather(packed, 'sx', axis=0, tiled=True)  38.3 us
    all_gather x1, blocking collectives, on_device(): lax.all_gather(token_expert, 'sx', axis=0, tiled=True)  21.3 us
    all_gather x1, blocking collectives, on_device(): lax.all_gather(priority, 'sx', axis=0, tiled=True)  14.5 us
    dot_general x1, matrix products, on_device(): jnp.dot(lax.all_gather(packed, 'sx', axis=0, tiled=True), gate_up_flat, p...  13.6 us
    unnamed x7, local copies, waits for them, and re-layouts  7.88 us
    dot_general x1, matrix products, on_device(): jnp.dot(activation_all, expert_down, preferred_element_type=jnp.float32)  7.63 us
  transfers between devices with their start and end apart: 2, of which 2 were waited for; matrix products, arithmetic and copies ran while one was open for 4% of the time, Pallas kernels for 0%

commit v1 on v0

v1 whole, which is shorter than its diff:
```python
import jax
import jax.numpy as jnp
from jax import lax
from jax.sharding import PartitionSpec as P

ROW_SCALE = 256.0
NO_TOKEN = 4096.0
LANES = 128


def expert_rows(rows, expert_gate_up, expert_down, count, chunk):
    devices, _, _ = rows.shape
    features, _, fr_dev = expert_gate_up.shape
    used = rows[:, :count, :features].reshape(devices * count, features)
    normed = (used.astype(jnp.float32) * (1.0 / ROW_SCALE)).astype(jnp.bfloat16)
    units = jnp.einsum("td,dgf->gtf", normed, expert_gate_up, preferred_element_type=jnp.float32)
    hidden = (jax.nn.silu(units[0]) * units[1]).astype(jnp.bfloat16).reshape(devices, count, fr_dev)
    if chunk <= count:
        hidden = hidden[:, :chunk]
    else:
        hidden = jnp.pad(hidden, ((0, 0), (0, chunk - count), (0, 0)))
    share = jnp.dot(
        hidden.reshape(devices * chunk, fr_dev), expert_down, preferred_element_type=jnp.float32
    ).astype(jnp.bfloat16)
    return lax.psum_scatter(share, "sx", scatter_dimension=0, tiled=True)


def on_device(hidden, norm_gain, route_expert, route_weight, priority, expert_gate_up, expert_down):
    devices = lax.axis_size("sx")
    tok_dev, features = hidden.shape
    slot_count = tok_dev // 2
    cap_rows = 3 * slot_count * devices // 8
    resid_float = hidden.astype(jnp.float32)
    scale_rows = lax.rsqrt(jnp.mean(resid_float * resid_float, axis=1, keepdims=True) + 1e-06)
    normed = (resid_float * scale_rows * norm_gain.astype(jnp.float32)[None, :]).astype(
        jnp.bfloat16
    )
    flight = route_expert[:, 0] == 0
    ahead = flight[None, :] & (priority[None, :] < priority[:, None])
    slot = jnp.sum(ahead.astype(jnp.int32), axis=1)
    selected = (jnp.arange(slot_count, dtype=jnp.int32)[:, None] == slot[None, :]) & flight[None, :]
    packed = jnp.dot(selected.astype(jnp.bfloat16), normed, preferred_element_type=jnp.float32)
    slot_priority = jnp.sum(
        jnp.where(selected, priority.astype(jnp.float32)[None, :] - NO_TOKEN, 0.0), axis=1
    )
    sent = jnp.concatenate(
        [
            (packed * ROW_SCALE).astype(jnp.float16),
            jnp.broadcast_to(
                (slot_priority + NO_TOKEN).astype(jnp.float16)[:, None], (slot_count, LANES)
            ),
        ],
        axis=1,
    )
    gathered = lax.all_gather(sent, "sx", axis=0, tiled=True)
    ranked = gathered[:, features].astype(jnp.float32)
    rank = jnp.sum((ranked[None, :] < ranked[:, None]).astype(jnp.int32), axis=1)
    kept = (ranked < NO_TOKEN) & (rank < cap_rows)
    kept_counts = jnp.sum(kept.reshape(devices, slot_count).astype(jnp.int32), axis=1)
    own_count = lax.dynamic_index_in_dim(kept_counts, lax.axis_index("sx"), keepdims=False)
    kept_local = flight & (slot < own_count)
    rows = gathered.reshape(devices, slot_count, features + LANES)

    def finish(returned):
        place = (
            (jnp.arange(returned.shape[0], dtype=jnp.int32)[None, :] == slot[:, None])
            & kept_local[:, None]
        ).astype(jnp.bfloat16)
        routed = jnp.dot(place, returned, preferred_element_type=jnp.float32)
        return (resid_float + route_weight[:, None] * routed).astype(jnp.bfloat16)

    few = 3 * slot_count // 4

    def narrow(rows):
        return finish(expert_rows(rows, expert_gate_up, expert_down, few, few - 1))

    def wide(rows):
        return finish(
            expert_rows(rows, expert_gate_up, expert_down, slot_count, slot_count + 15)
        )

    return lax.cond(jnp.max(kept_counts) < few, narrow, wide, rows)


def solution(mesh):
    in_specs = (
        P(("dp", "sx"), None),
        P(),
        P(("dp", "sx"), None),
        P(("dp", "sx")),
        P(("dp", "sx")),
        P(None, None, "sx"),
        P("sx", None),
    )
    out_specs = P(("dp", "sx"), None)
    return jax.shard_map(
        on_device, mesh=mesh, in_specs=in_specs, out_specs=out_specs, check_vma=False
    )
```

time: 192 us -> 132 us (0.69)
  waiting for transfers between devices: 101 us -> 0.53 us
  blocking collectives: 35.8 us -> 86.8 us
  between operations: 13.5 us -> 0.77 us
  matrix products: 23.6 us -> 17.4 us
  other arithmetic: 6.95 us -> 12.1 us
    reduce_scatter x1 -> x0, waiting for transfers between devices: 62.3 us -> none  [on_device(): lax.psum_scatter(jnp.dot(activation_all, expert_down, preferred_element_t...]
    all_gather x1 -> x0, waiting for transfers between devices: 38.3 us -> none  [on_device(): lax.all_gather(packed, 'sx', axis=0, tiled=True)]
    unnamed x0 -> x1, blocking collectives: none -> 36.5 us
    all_gather x2 -> x1, blocking collectives: 35.8 us -> 50.3 us  [on_device(): gathered = lax.all_gather(sent, 'sx', axis=0, tiled=True)]
    dot_general x3 -> x4, matrix products: 23.6 us -> 17.4 us  [the longest x1 8.67 us: expert_rows(): jnp.dot(hidden.reshape(devices * chunk, fr_dev), expert_down, preferred_e...]
    convert_element_type x2 -> x5, other arithmetic: 2.41 us -> 5.29 us  [the longest x1 3.46 us: expert_rows(): normed = (used.astype(jnp.float32) * (1.0 / ROW_SCALE)).astype(jnp.bfloat16)]
    unnamed x0 -> x1, starting transfers between devices: none -> 1.92 us
    unnamed x7 -> x15, local copies, waits for them, and re-layouts: 7.88 us -> 8.11 us
  transfers between devices with their start and end apart: 2 -> 1, of which waited for: 2 -> 1; matrix products, arithmetic and copies ran while one was open for 4% -> 1% of each run, Pallas kernels for 0% -> 0%
where the time goes in v1:
time: 132 us; the launch traced here: 131 us
  blocking collectives  86.8 us (66%)
  matrix products  17.4 us (13%)
  other arithmetic  12.1 us (9%)
  local copies, waits for them, and re-layouts  10.5 us (8%)
  starting transfers between devices  1.92 us (1%)
    all_gather x1, blocking collectives, on_device(): gathered = lax.all_gather(sent, 'sx', axis=0, tiled=True)  50.3 us
    unnamed x1, blocking collectives  36.5 us
    dot_general x1, matrix products, expert_rows(): jnp.dot(hidden.reshape(devices * chunk, fr_dev), expert_down, preferred_e...  8.67 us
    unnamed x15, local copies, waits for them, and re-layouts  8.11 us
    dot_general x1, matrix products, expert_rows(): jnp.einsum('td,dgf->gtf', normed, expert_gate_up, preferred_element_type=...  6.75 us
    convert_element_type x1, other arithmetic, expert_rows(): normed = (used.astype(jnp.float32) * (1.0 / ROW_SCALE)).astype(jnp.bfloat16)  3.46 us
  transfers between devices with their start and end apart: 1, of which 1 were waited for; matrix products, arithmetic and copies ran while one was open for 1% of the time, Pallas kernels for 0%

profile of v1, /device:TPU:1, one launch (start us, length us, event | category | flops | bytes accessed | tf_op | source)
XLA Modules:
  0.0 131.1 jit_solution(4263585828896155871)
XLA Ops:
  0.0 0.7 convert_add_fusion
  0.7 0.7 compare_bitcast_fusion
  1.3 0.9 convert_reduce_fusion.2
  2.2 0.1 select_reduce_fusion
  2.4 0.7 convert_element_type.110
  3.1 1.4 %multiply_reduce_fusion = f32[128]{0:T(128)S(1)} fusion(bf16[128,3200]{1,0:T(8,128)(2,1)} %param.9), kind=kLoop, calls=%fused_computation.39 | loop fusion | flops 1228672 | bytes 819712 | tf_op jit(solution)/shard_map/reduce_sum | solution.py:34
  4.5 1.6 %fusion.29 = f16[64,3200]{1,0:T(8,128)(2,1)S(1)} fusion(f32[3200]{0:T(1024)S(1)} %convert_element_type.110, f32[128]{0:T(128)S(1)} %add_rsqrt_fusion, bf16[128,3200]{1,0:T(8,128)(2,1)} %param.9, s32[128]{0:T(128)S(1)} %convert_reduce_fusion.2, pred[128]{0:T(512)(128)(4,1)S(1)} %compare_bitcast_fusion), kind=kOutput, calls=%fused_computation.36 | convolution fusion | flops 54493184 | bytes 1242752 | tf_op jit(solution)/shard_map/dot_general | solution.py:42
  6.3 50.3 %all-gather.1 = f16[1024,3328]{1,0:T(8,128)(2,1)S(1)} all-gather(f16[64,3328]{1,0:T(8,128)(2,1)S(1)} %pad_maximum_fusion), channel_id=1, replica_groups=mesh['dp'=16,'sx'=16] {'sx'}, dimensions={0}, use_global_device_ids=true | all-gather | bytes 7241728 | tf_op jit(solution)/shard_map/all_gather | solution.py:55
  56.6 2.8 %copy-done = f16[1024,3328]{1,0:T(8,128)(2,1)} copy-done((f16[1024,3328]{1,0:T(8,128)(2,1)}, f16[1024,3328]{1,0:T(8,128)(2,1)S(1)}, u32[]{:S(2)}) %copy-start) | copy-done | bytes 6815768
  59.4 0.2 fusion.33
  59.7 1.2 convert_reduce_fusion.1
  60.9 0.6 convert_reduce_fusion
  61.5 0.1 convert_reduce_fusion.3
  61.6 0.6 reduce_max.9
  63.1 67.1 %conditional.7 = (bf16[128,3200]{1,0:T(8,128)(2,1)S(1)}) conditional(s32[]{:T(128)} %convert_element_type.120, (f32[128]{0:T(128)S(1)}, s32[128]{0:T(128)S(1)}, s32[]{:T(128)}, s32[16]{0:T(128)S(1)}, pred[128]{0:T(512)(128)(4,1)S(1)}, /*index=5*/f16[1024,3328]{1,0:T(8,128)(2,1)}, bf16[3200,2,640]{2,1,0:T(2,128)(2,1)}, bf16[640,3200]{1,0:T(8,128)(2,1)}, ...), branch_computations={%region_6.8_spmd, %region_8.10_spmd} | conditional | flops 13653821440 | bytes 116241864
  63.3 3.5 %multiply_convert_fusion.2 = bf16[16,48,3200]{2,1,0:T(8,128)(2,1)S(1)} fusion(f16[16,64,3328]{2,1,0:T(8,128)(2,1)} %bitcast.33), kind=kLoop, calls=%fused_computation.15 | loop fusion | flops 7372800 | bytes 9830400 | tf_op jit(solution)/shard_map/cond/branch_1_fun/convert_element_type | solution.py:15
  66.8 1.3 %copy-done.7 = bf16[3200,2,640]{2,1,0:T(2,128)(2,1)S(1)} copy-done((bf16[3200,2,640]{2,1,0:T(2,128)(2,1)S(1)}, bf16[3200,2,640]{2,1,0:T(2,128)(2,1)}, u32[]{:S(2)}) %copy-start.7) | copy-done | bytes 8192024
  68.1 6.7 %fusion.17 = f32[2,768,640]{2,1,0:T(8,128)S(1)} fusion(bf16[768,3200,1]{1,0,2:T(8,128)(2,1)S(1)} %bitcast.40, bf16[3200,2,640]{2,1,0:T(2,128)(2,1)S(1)} %copy-done.7), kind=kOutput, calls=%fused_computation.21 | convolution fusion | flops 6291456000 | bytes 17039360 | tf_op jit(solution)/shard_map/cond/branch_1_fun/td,dgf->gtf/dot_general | solution.py:16
  74.8 0.3 fusion.39
  75.1 0.1 neg.9
  75.2 0.6 fusion.20
  75.8 1.3 reshape.78
  77.1 8.7 %convolution_convert_fusion.1 = bf16[752,3200]{1,0:T(8,128)(2,1)} fusion(bf16[752,640]{1,0:T(8,128)(2,1)} %reshape.78, bf16[640,3200]{1,0:T(8,128)(2,1)} %get-tuple-element.108), kind=kOutput, calls=%fused_computation.18 | convolution fusion | flops 3082598400 | bytes 9871360 | tf_op jit(solution)/shard_map/cond/branch_1_fun/dot_general | solution.py:22
  85.8 36.5 %fusion.1 = bf16[48,3200]{1,0:T(8,128)(2,1)S(1)} fusion(bf16[752,3200]{1,0:T(8,128)(2,1)} %convolution_convert_fusion.1), kind=kCustom, calls=%all-reduce-scatter.1 | all-reduce-scatter fusion | flops 2457601 | bytes 5121024
  122.3 1.9 %collective-permute-start.1 = (bf16[15,3200]{1,0:T(8,128)(2,1)S(1)}, bf16[15,3200]{1,0:T(8,128)(2,1)S(1)}, u32[]{:S(2)}, u32[]{:S(2)}) collective-permute-start(bf16[15,3200]{1,0:T(8,128)(2,1)S(1)} %slice.36), channel_id=1, source_target_pairs={{0,1},{1,2},{2,3},{3,4},{4,5},{5,6},{6,7},{7,8},{8,9},{9,10},{10,1... | collective-permute-start | bytes 288008
  124.3 0.7 dynamic_slice.7
  124.9 0.6 compare_and_fusion.1
  125.6 0.6 dynamic-slice.10
  126.8 0.5 collective-permute-done.1
  127.4 2.4 %concatenate.5 = bf16[63,3200]{1,0:T(8,128)(2,1)S(1)} concatenate(bf16[15,3200]{1,0:T(8,128)(2,1)S(1)} %collective-permute-done.1, bf16[48,3200]{1,0:T(8,128)(2,1)S(1)} %fusion.1), dimensions={0} | concatenate | bytes 806400
  129.7 0.4 fusion.16
  130.2 0.9 copy-done.2
  (18 shorter events, 0.5 us)
Async XLA Ops:
  6.2 56.7 %copy-start.1 = (bf16[128,3200]{1,0:T(8,128)(2,1)S(1)}, bf16[128,3200]{1,0:T(8,128)(2,1)}, u32[]{:S(2)}) copy-start(bf16[128,3200]{1,0:T(8,128)(2,1)} %param.9) | copy-start | bytes 2457604
  6.2 56.8 %copy-start.3 = (f32[128]{0:T(128)S(1)}, f32[128]{0:T(128)}, u32[]{:S(2)}) copy-start(f32[128]{0:T(128)} %param.12) | copy-start | bytes 1540
  56.6 2.8 %copy-start = (f16[1024,3328]{1,0:T(8,128)(2,1)}, f16[1024,3328]{1,0:T(8,128)(2,1)S(1)}, u32[]{:S(2)}) copy-start(f16[1024,3328]{1,0:T(8,128)(2,1)S(1)} %all-gather.1) | copy-start | bytes 20447236
  63.3 4.8 %copy-start.7 = (bf16[3200,2,640]{2,1,0:T(2,128)(2,1)S(1)}, bf16[3200,2,640]{2,1,0:T(2,128)(2,1)}, u32[]{:S(2)}) copy-start(bf16[3200,2,640]{2,1,0:T(2,128)(2,1)} %get-tuple-element.178) | copy-start | bytes 24576004
  85.8 39.8 %copy-start.5 = (u32[256]{0:T(256)S(1)}, u32[256]{0:T(256)}, u32[]{:S(2)}) copy-start(u32[256]{0:T(256)} %constant.63) | copy-start | bytes 3076
  122.3 5.0 %collective-permute-start.1 = (bf16[15,3200]{1,0:T(8,128)(2,1)S(1)}, bf16[15,3200]{1,0:T(8,128)(2,1)S(1)}, u32[]{:S(2)}, u32[]{:S(2)}) collective-permute-start(bf16[15,3200]{1,0:T(8,128)(2,1)S(1)} %slice.36), channel_id=1, source_target_pairs={{0,1},{1,2},{2,3},{3,4},{4,5},{5,6},{6,7},{7,8},{8,9},{9,10},{10,1... | collective-permute-start | bytes 288008
  130.2 0.9 copy-start.2

commit v2 on v0

v2 whole, which is shorter than its diff:
```python
import functools

import jax
import jax.numpy as jnp
from jax import lax
from jax.experimental import pallas as pl
from jax.experimental.pallas import tpu as pltpu
from jax.sharding import PartitionSpec as P

ROW_SCALE = 256.0
NO_TOKEN = 4096
RADIX = 64
LANES = 128
COLUMNS = 1280
VMEM = pltpu.VMEM


def as_column(row):
    n = row.shape[1]
    square = lax.broadcasted_iota(jnp.int32, (n, n), 0) == lax.broadcasted_iota(
        jnp.int32, (n, n), 1
    )
    return jnp.sum(jnp.where(square, row, jnp.zeros_like(row)), axis=1, keepdims=True)


def pack_kernel(
    hidden_ref, gain_ref, expert_ref, priority_ref, weight_ref,
    first_ref, all_ref, slot_ref, asked_ref, scale_ref,
):
    slots = all_ref.shape[0]
    few = first_ref.shape[0]
    tokens = hidden_ref.shape[0]
    flight = (expert_ref[...] == 0).astype(jnp.float32)
    priority = priority_ref[...].astype(jnp.float32)
    own = jnp.where(flight > 0, priority, float(NO_TOKEN))
    own_column = as_column(own)
    slot_row = jnp.sum((own_column < own).astype(jnp.float32), axis=0, keepdims=True)
    slot_column = jnp.sum((own < own_column).astype(jnp.float32), axis=1, keepdims=True)
    slot_row = jnp.where(flight > 0, slot_row, float(slots))
    slot_column = jnp.where(own_column < NO_TOKEN, slot_column, float(slots))
    slot_ref[...] = slot_row.astype(jnp.int32)
    asked_ref[...] = own_column
    scale_ref[...] = as_column(weight_ref[...])

    resid = hidden_ref[...].astype(jnp.float32)
    scale = lax.rsqrt(jnp.mean(resid * resid, axis=1, keepdims=True) + 1e-06)
    normed = (resid * scale * gain_ref[...].astype(jnp.float32)).astype(jnp.bfloat16)
    place = lax.broadcasted_iota(jnp.int32, (slots, tokens), 0).astype(jnp.float32) == slot_row
    selector = jnp.where(place, ROW_SCALE, 0.0).astype(jnp.bfloat16)
    packed = jnp.dot(selector, normed, preferred_element_type=jnp.float32)
    all_ref[...] = packed.astype(jnp.bfloat16)

    lane = lax.broadcasted_iota(jnp.int32, (tokens, LANES), 1)
    holds = lax.rem(lane, slots).astype(jnp.float32) == slot_column
    held = NO_TOKEN + jnp.sum(
        jnp.where(holds, own_column - NO_TOKEN, 0.0), axis=0, keepdims=True
    )
    quotient = jnp.floor(held * (1.0 / RADIX))
    low = lax.broadcasted_iota(jnp.int32, (1, LANES), 1) < slots
    code = jnp.where(low, quotient, held - quotient * RADIX)
    row = lax.broadcasted_iota(jnp.int32, (few, LANES), 0)
    first_ref[:, LANES:] = packed[:few, LANES:].astype(jnp.bfloat16)
    first_ref[:, :LANES] = jnp.where(row == few - 1, code, packed[:few, :LANES]).astype(
        jnp.bfloat16
    )


def pack(hidden, norm_gain, route_expert, priority, route_weight):
    tokens, features = hidden.shape
    slots = tokens // 2
    few = 3 * slots // 4
    return pl.pallas_call(
        pack_kernel,
        out_shape=(
            jax.ShapeDtypeStruct((few, features), jnp.bfloat16),
            jax.ShapeDtypeStruct((slots, features), jnp.bfloat16),
            jax.ShapeDtypeStruct((1, tokens), jnp.int32),
            jax.ShapeDtypeStruct((tokens, 1), jnp.float32),
            jax.ShapeDtypeStruct((tokens, 1), jnp.float32),
        ),
        compiler_params=pltpu.CompilerParams(vmem_limit_bytes=16 * 1024 * 1024),
    )(
        hidden,
        norm_gain.reshape(1, features),
        route_expert.reshape(1, tokens),
        priority.reshape(1, tokens),
        route_weight.reshape(1, tokens),
    )


def down_kernel(
    devices, cap_rows, units_ref, down_ref, rows_ref, asked_ref, scale_ref,
    share_ref, weight_ref, many_ref, spread_ref, hidden_ref,
):
    count = units_ref.shape[1] // devices
    chunk = share_ref.shape[0] // devices

    @pl.when(pl.program_id(0) == 0)
    def _():
        for device in range(devices):
            rows = pl.ds(device * count, count)
            gate = units_ref[0, rows, :] * (1.0 / ROW_SCALE)
            up = units_ref[1, rows, :] * (1.0 / ROW_SCALE)
            spread_ref[pl.ds(device * chunk, count), :] = gate * up / (1.0 + jnp.exp(-gate))
        hidden_ref[...] = spread_ref[: devices * chunk, :].astype(jnp.bfloat16)

        slots = LANES // 2
        lane = lax.broadcasted_iota(jnp.int32, (1, LANES), 1)
        asked = asked_ref[...]
        ahead = jnp.zeros((asked.shape[0], LANES), jnp.float32)
        held = []
        for device in range(devices):
            tile = rows_ref[pl.ds(device * count + count - 16, 16), :LANES].astype(jnp.float32)
            code = tile[15:16, :]
            whole = jnp.where(lane < slots, code * RADIX + pltpu.roll(code, slots, 1), 2.0 * NO_TOKEN)
            held.append(whole)
            ahead += (whole < asked).astype(jnp.float32)
        rank = jnp.sum(ahead, axis=1, keepdims=True)
        weight_ref[...] = jnp.where(
            (asked < NO_TOKEN) & (rank < cap_rows), scale_ref[...], 0.0
        )
        table = jnp.concatenate(held, axis=0)
        last = jnp.sum(
            jnp.where(lax.broadcasted_iota(jnp.int32, table.shape, 1) == count - 1, table, 0.0),
            axis=1,
            keepdims=True,
        )
        ahead = jnp.zeros((devices, LANES), jnp.float32)
        for whole in held:
            ahead += (whole < last).astype(jnp.float32)
        rank = jnp.sum(ahead, axis=1, keepdims=True)
        many = jnp.where((last < NO_TOKEN) & (rank < cap_rows), 1.0, 0.0)
        many_ref[0, 0] = jnp.max(many).astype(jnp.int32)

    share_ref[...] = jnp.dot(
        hidden_ref[...], down_ref[...], preferred_element_type=jnp.float32
    ).astype(jnp.bfloat16)


def down_share(units, expert_down, rows, asked, scale, devices, cap_rows):
    _, slots, fr_dev = units.shape
    features = expert_down.shape[1]
    count = slots // devices
    chunks = devices * (count - 1)
    return pl.pallas_call(
        functools.partial(down_kernel, devices, cap_rows),
        grid=(pl.cdiv(features, COLUMNS),),
        in_specs=[
            pl.BlockSpec(memory_space=VMEM),
            pl.BlockSpec((fr_dev, COLUMNS), lambda i: (0, i)),
            pl.BlockSpec((slots, LANES), lambda i: (0, 0)),
            pl.BlockSpec(memory_space=VMEM),
            pl.BlockSpec(memory_space=VMEM),
        ],
        out_specs=(
            pl.BlockSpec((chunks, COLUMNS), lambda i: (0, i)),
            pl.BlockSpec(asked.shape, lambda i: (0, 0)),
            pl.BlockSpec(memory_space=pltpu.SMEM),
        ),
        out_shape=(
            jax.ShapeDtypeStruct((chunks, features), jnp.bfloat16),
            jax.ShapeDtypeStruct(asked.shape, jnp.float32),
            jax.ShapeDtypeStruct((1, 1), jnp.int32),
        ),
        scratch_shapes=[
            VMEM((slots, fr_dev), jnp.float32),
            VMEM((chunks, fr_dev), jnp.bfloat16),
        ],
        compiler_params=pltpu.CompilerParams(vmem_limit_bytes=28 * 1024 * 1024),
        cost_estimate=pl.CostEstimate(
            flops=2 * chunks * fr_dev * features,
            bytes_accessed=2 * fr_dev * features + 2 * chunks * features,
            transcendentals=slots * fr_dev,
        ),
    )(units, expert_down, rows, asked, scale)


def expert_units(rows, expert_gate_up):
    return jnp.einsum("td,dgf->gtf", rows, expert_gate_up, preferred_element_type=jnp.float32)


def wide_share(rows, expert_gate_up, expert_down, chunk):
    devices, count, features = rows.shape
    fr_dev = expert_down.shape[0]
    normed = rows.reshape(devices * count, features).astype(jnp.bfloat16)
    units = expert_units(normed, expert_gate_up) * (1.0 / ROW_SCALE)
    hidden = (jax.nn.silu(units[0]) * units[1]).astype(jnp.bfloat16)
    hidden = jnp.pad(
        hidden.reshape(devices, count, fr_dev), ((0, 0), (0, chunk - count), (0, 0))
    )
    return jnp.dot(
        hidden.reshape(devices * chunk, fr_dev), expert_down, preferred_element_type=jnp.float32
    ).astype(jnp.bfloat16)


def on_device(hidden, norm_gain, route_expert, route_weight, priority, expert_gate_up, expert_down):
    devices = lax.axis_size("sx")
    tok_dev = hidden.shape[0]
    slot_count = tok_dev // 2
    cap_rows = 3 * slot_count * devices // 8
    first, every, slot, asked, scale = pack(
        hidden, norm_gain, route_expert, priority, route_weight
    )
    gathered = lax.all_gather(first.astype(jnp.float16), "sx", axis=0, tiled=True)
    rows = lax.optimization_barrier(gathered.astype(jnp.bfloat16))
    units = expert_units(rows, expert_gate_up)
    share, weight, many = down_share(
        units, expert_down, rows, asked, scale, devices, cap_rows
    )

    def finish(returned):
        place = (
            jnp.arange(returned.shape[0], dtype=jnp.int32)[None, :] == slot.reshape(tok_dev, 1)
        ).astype(jnp.bfloat16)
        routed = jnp.dot(place, returned, preferred_element_type=jnp.float32)
        return (hidden.astype(jnp.float32) + weight * routed).astype(jnp.bfloat16)

    def narrow(share, every):
        return finish(lax.psum_scatter(share, "sx", scatter_dimension=0, tiled=True))

    def wide(share, every):
        rows = lax.all_gather(every.astype(jnp.float16), "sx", axis=0, tiled=False)
        share = wide_share(rows, expert_gate_up, expert_down, slot_count + 15)
        return finish(lax.psum_scatter(share, "sx", scatter_dimension=0, tiled=True))

    return lax.cond(many[0, 0] > 0, wide, narrow, share, every)


def solution(mesh):
    in_specs = (
        P(("dp", "sx"), None),
        P(),
        P(("dp", "sx"), None),
        P(("dp", "sx")),
        P(("dp", "sx")),
        P(None, None, "sx"),
        P("sx", None),
    )
    out_specs = P(("dp", "sx"), None)
    return jax.shard_map(
        on_device, mesh=mesh, in_specs=in_specs, out_specs=out_specs, check_vma=False
    )
```

time: 192 us -> 107 us (0.56); the launches traced: 190 us -> 107 us
  waiting for transfers between devices: 101 us -> 1.79 us
  blocking collectives: 35.8 us -> 76.4 us
  matrix products: 23.6 us -> 8.07 us
  between operations: 13.5 us -> 0.73 us
  Pallas kernels: 0 us -> 9.43 us
  other arithmetic: 6.95 us -> 0.73 us
  local copies, waits for them, and re-layouts: 9.13 us -> 7.19 us
    reduce_scatter x1 -> x0, waiting for transfers between devices: 62.3 us -> none  [on_device(): lax.psum_scatter(jnp.dot(activation_all, expert_down, preferred_element_t...]
    all_gather x1 -> x0, waiting for transfers between devices: 38.3 us -> none  [on_device(): lax.all_gather(packed, 'sx', axis=0, tiled=True)]
    unnamed x0 -> x1, blocking collectives: none -> 36.4 us
    dot_general x3 -> x2, matrix products: 23.6 us -> 8.07 us  [the longest x1 6.75 us: expert_units(): jnp.einsum('td,dgf->gtf', rows, expert_gate_up, preferred_element_type=jn...]
    pallas_call x0 -> x2, Pallas kernels: none -> 9.43 us  [the longest x1 7.75 us: down_share(): pl.pallas_call(functools.partial(down_kernel, devices, cap_rows), grid=(p...]
    all_gather x2 -> x1, blocking collectives: 35.8 us -> 39.9 us  [on_device(): lax.all_gather(first.astype(jnp.float16), 'sx', axis=0, tiled=True)]
    reduce_sum x3 -> x0, other arithmetic: 2.43 us -> none  [the longest x1 1.39 us: on_device(): jnp.mean(resid_float * resid_float, axis=1, keepdims=True) + 1e-06]
    convert_element_type x3 -> x2, other arithmetic: 3.12 us -> 0.73 us  [the longest x1 0.67 us: on_device(): rows = lax.optimization_barrier(gathered.astype(jnp.bfloat16))]
  transfers between devices with their start and end apart: 2 -> 1, of which waited for: 2 -> 1; matrix products, arithmetic and copies ran while one was open for 4% -> 1% of each run, Pallas kernels for 0% -> 0%
where the time goes in v2:
time: 107 us
  blocking collectives  76.4 us (71%)
  Pallas kernels  9.43 us (9%)
  matrix products  8.07 us (8%)
  local copies, waits for them, and re-layouts  7.19 us (7%)
  starting transfers between devices  1.92 us (2%)
  waiting for transfers between devices  1.79 us (2%)
    all_gather x1, blocking collectives, on_device(): lax.all_gather(first.astype(jnp.float16), 'sx', axis=0, tiled=True)  39.9 us
    unnamed x1, blocking collectives  36.4 us
    pallas_call x1, Pallas kernels, down_share(): pl.pallas_call(functools.partial(down_kernel, devices, cap_rows), grid=(p...  7.75 us
    dot_general x1, matrix products, expert_units(): jnp.einsum('td,dgf->gtf', rows, expert_gate_up, preferred_element_type=jn...  6.75 us
    unnamed x19, local copies, waits for them, and re-layouts  6.42 us
  transfers between devices with their start and end apart: 1, of which 1 were waited for; matrix products, arithmetic and copies ran while one was open for 1% of the time, Pallas kernels for 0%

profile of v2, /device:TPU:1, one launch (start us, length us, event | category | flops | bytes accessed | tf_op | source)
XLA Modules:
  0.0 106.9 jit_solution(14937798024981536137)
XLA Ops:
  0.0 0.7 reshape.28.gain_ref
  0.7 0.0 copy-start
  0.7 0.6 copy-done
  1.4 0.0 copy-start.1
  1.4 0.7 copy-done.1
  2.0 0.0 copy-start.2
  2.0 0.7 copy-done.2
  2.7 1.7 %shard_map.75 = (bf16[48,3200]{1,0:T(8,128)(2,1)S(1)}, bf16[64,3200]{1,0:T(8,128)(2,1)S(1)}, s32[1,128]{1,0:T(1,128)S(1)}, f32[128,1]{1,0:T(8,128)S(1)}, f32[128,1]{1,0:T(8,128)S(1)}) custom-call(bf16[128,3200]{1,0:T(8,128)(2,1)} %hidden_ref.1, bf16[1,3200]{1,0:T(2,128)(2,1)S(1)} %reshape.28.gain_ref, s32[1,128]{1,0:T(1,128)S(1)} %bitcast.32, ...), custom_call_target="tpu_custom_call" | custom-call | tf_op jit(solution)/shard_map/pallas_call | solution.py:72
  4.4 0.1 convert_element_type.50
  4.4 0.0 slice-start
  4.4 39.9 %all-gather.4 = f16[768,3200]{1,0:T(8,128)(2,1)S(1)} all-gather(f16[48,3200]{1,0:T(8,128)(2,1)S(1)} %convert_element_type.50), channel_id=1, replica_groups=mesh['dp'=16,'sx'=16] {'sx'}, dimensions={0}, use_global_device_ids=true | all-gather | bytes 5222400 | tf_op jit(solution)/shard_map/all_gather | solution.py:204
  44.4 0.0 slice-start.1
  44.4 0.7 convert_element_type.51.rows_ref
  45.1 0.0 slice-done
  45.1 1.4 %slice-done.1 = s8[3997696]{0:T(1024)(128)(4,1)S(1)} async-done(((s8[8192000]{0:T(1024)(128)(4,1)}), s8[3997696]{0:T(1024)(128)(4,1)S(1)}, s32[]{:S(2)}) %slice-start.1) | async-done | bytes 3997720
  46.5 0.0 copy-start.4
  46.5 6.8 %fusion.21.units_ref = f32[2,768,640]{2,1,0:T(8,128)S(1)} fusion(bf16[3200,2,640]{2,1,0:T(2,128)(2,1)S(1)} %bitcast.42, bf16[768,3200]{1,0:T(8,128)(2,1)S(1)} %convert_element_type.51.rows_ref), kind=kOutput, calls=%fused_computation.22 | convolution fusion | flops 6291456000 | bytes 17039360 | tf_op jit(solution)/shard_map/td,dgf->gtf/dot_general | solution.py:179
  53.3 0.0 copy-done.4
  53.3 0.0 copy-start.3
  53.3 7.7 %shard_map.76 = (bf16[752,3200]{1,0:T(8,128)(2,1)}, f32[128,1]{1,0:T(8,128)S(1)}, s32[1,1]{1,0:T(1,128)}) custom-call(f32[2,768,640]{2,1,0:T(8,128)S(1)} %fusion.21.units_ref, bf16[640,3200]{1,0:T(8,128)(2,1)S(1)} %copy-done.4, bf16[768,3200]{1,0:T(8,128)(2,1)S(1)} %convert_element_type.51.rows_ref, f32[128,1]{1,0:T(8,128)S(1)} %get-tuple-element.53.asked_ref, ...), custom_call_target="tpu_custom_call" | custom-call | flops 3080192000 | bytes 8908800 | tf_op jit(solution)/shard_map/pallas_call | solution.py:145
  61.7 0.0 copy-done.3
  61.7 45.2 %conditional.7 = (bf16[128,3200]{1,0:T(8,128)(2,1)}) conditional(s32[]{:T(128)} %bitcast.13, (bf16[128,3200]{1,0:T(8,128)(2,1)S(1)}, f32[128,1]{1,0:T(8,128)S(1)}, s32[1,128]{1,0:T(1,128)S(1)}, bf16[752,3200]{1,0:T(8,128)(2,1)}) %tuple.37, (bf16[128,3200]{1,0:T(8,128)(2,1)S(1)}, f32[128,1]{1,0:T(8,128)S(1)}, s32[1,128]{1,0:T(1,128)S(1)}, ...), branch_computations={%region_0.0_spmd, %region_2.4_spmd} | conditional | flops 13649182720 | bytes 136967360
  61.7 0.0 copy-start.7
  61.7 36.4 %fusion = bf16[48,3200]{1,0:T(8,128)(2,1)S(1)} fusion(bf16[752,3200]{1,0:T(8,128)(2,1)} %get-tuple-element.37), kind=kCustom, calls=%all-reduce-scatter | all-reduce-scatter fusion | flops 2457601 | bytes 5121024
  98.2 1.9 %collective-permute-start = (bf16[15,3200]{1,0:T(8,128)(2,1)S(1)}, bf16[15,3200]{1,0:T(8,128)(2,1)S(1)}, u32[]{:S(2)}, u32[]{:S(2)}) collective-permute-start(bf16[15,3200]{1,0:T(8,128)(2,1)S(1)} %slice.8), channel_id=1, source_target_pairs={{0,1},{1,2},{2,3},{3,4},{4,5},{5,6},{6,7},{7,8},{8,9},{9,10},{10,1... | collective-permute-start | bytes 288008
  100.1 0.1 copy.23
  100.2 0.0 copy-done.7
  100.2 0.6 dynamic-slice.6
  101.4 1.8 %collective-permute-done = bf16[15,3200]{1,0:T(8,128)(2,1)S(1)} collective-permute-done((bf16[15,3200]{1,0:T(8,128)(2,1)S(1)}, bf16[15,3200]{1,0:T(8,128)(2,1)S(1)}, u32[]{:S(2)}, u32[]{:S(2)}) %collective-permute-start) | collective-permute-done | bytes 96032
  103.2 2.4 %concatenate = bf16[63,3200]{1,0:T(8,128)(2,1)S(1)} concatenate(bf16[15,3200]{1,0:T(8,128)(2,1)S(1)} %collective-permute-done, bf16[48,3200]{1,0:T(8,128)(2,1)S(1)} %fusion), dimensions={0} | concatenate | bytes 806400
  105.6 1.3 %fusion.2 = bf16[128,3200]{1,0:T(8,128)(2,1)} fusion(bf16[128,3200]{1,0:T(8,128)(2,1)S(1)} %get-tuple-element.34, f32[128]{0:T(128)S(1)} %bitcast.37, bf16[63,3200]{1,0:T(8,128)(2,1)S(1)} %concatenate, u32[]{:S(6)} %subtract, s32[128]{0:T(128)S(1)} %bitcast.38), kind=kOutput, calls=%fused_computation.1 | convolution fusion | flops 40146816 | bytes 1946628 | tf_op jit(solution)/shard_map/cond/branch_0_fun/dot_general | solution.py:215
  (2 shorter events, 0.0 us)
Async XLA Ops:
  0.7 0.7 copy-start
  1.4 0.7 copy-start.1
  2.0 0.7 copy-start.2
  4.4 40.6 %slice-start = ((s8[8192000]{0:T(1024)(128)(4,1)}), s8[4194304]{0:T(1024)(128)(4,1)S(1)}, s32[]{:S(2)}) async-start(s8[8192000]{0:T(1024)(128)(4,1)} %bitcast.41), calls=%async_computation | async-start | bytes 8388608
  44.4 2.1 %slice-start.1 = ((s8[8192000]{0:T(1024)(128)(4,1)}), s8[3997696]{0:T(1024)(128)(4,1)S(1)}, s32[]{:S(2)}) async-start(s8[8192000]{0:T(1024)(128)(4,1)} %bitcast.41), calls=%async_computation.1 | async-start | bytes 7995392
  46.5 6.8 %copy-start.4 = (bf16[640,3200]{1,0:T(8,128)(2,1)S(1)}, bf16[640,3200]{1,0:T(8,128)(2,1)}, u32[]{:S(2)}) copy-start(bf16[640,3200]{1,0:T(8,128)(2,1)} %down_ref.1) | copy-start | bytes 12288004
  53.3 8.4 %copy-start.3 = (bf16[128,3200]{1,0:T(8,128)(2,1)S(1)}, bf16[128,3200]{1,0:T(8,128)(2,1)}, u32[]{:S(2)}) copy-start(bf16[128,3200]{1,0:T(8,128)(2,1)} %hidden_ref.1) | copy-start | bytes 2457604
  61.7 38.5 %copy-start.7 = (u32[256]{0:T(256)S(1)}, u32[256]{0:T(256)}, u32[]{:S(2)}) copy-start(u32[256]{0:T(256)} %constant.19) | copy-start | bytes 3076
  98.2 5.0 %collective-permute-start = (bf16[15,3200]{1,0:T(8,128)(2,1)S(1)}, bf16[15,3200]{1,0:T(8,128)(2,1)S(1)}, u32[]{:S(2)}, u32[]{:S(2)}) collective-permute-start(bf16[15,3200]{1,0:T(8,128)(2,1)S(1)} %slice.8), channel_id=1, source_target_pairs={{0,1},{1,2},{2,3},{3,4},{4,5},{5,6},{6,7},{7,8},{8,9},{9,10},{10,1... | collective-permute-start | bytes 288008

commit v3 on v2

v3 whole, which is shorter than its diff:
```python
import functools

import jax
import jax.numpy as jnp
from jax import lax
from jax.experimental import pallas as pl
from jax.experimental.pallas import tpu as pltpu
from jax.sharding import PartitionSpec as P

ROW_SCALE = 256.0
NO_TOKEN = 4096
RADIX = 64
LANES = 128
ROW_BLOCK = 256
VMEM = pltpu.VMEM


def as_column(row):
    n = row.shape[1]
    square = lax.broadcasted_iota(jnp.int32, (n, n), 0) == lax.broadcasted_iota(
        jnp.int32, (n, n), 1
    )
    return jnp.sum(jnp.where(square, row, jnp.zeros_like(row)), axis=1, keepdims=True)


def pack_kernel(
    hidden_hbm, gain_hbm, own_hbm, first_ref, all_ref, slot_ref, asked_ref,
    hidden_ref, gain_ref, own_ref, arrived,
):
    copies = [
        pltpu.make_async_copy(source, target, arrived.at[i])
        for i, (source, target) in enumerate(
            (
                (own_hbm, own_ref),
                (gain_hbm, gain_ref),
                (hidden_hbm, hidden_ref),
            )
        )
    ]
    for copy in copies:
        copy.start()
    for copy in copies[:2]:
        copy.wait()
    slots, features = all_ref.shape
    few = first_ref.shape[0]
    tokens = hidden_ref.shape[0]
    own = own_ref[...]
    own_column = as_column(own)
    slot_row = jnp.sum((own_column < own).astype(jnp.float32), axis=0, keepdims=True)
    slot_column = jnp.sum((own < own_column).astype(jnp.float32), axis=1, keepdims=True)
    slot_row = jnp.where(own < NO_TOKEN, slot_row, float(slots))
    slot_column = jnp.where(own_column < NO_TOKEN, slot_column, float(slots))
    slot_ref[...] = slot_row.astype(jnp.int32)
    asked_ref[...] = own_column
    place = lax.broadcasted_iota(jnp.int32, (slots, tokens), 0).astype(jnp.float32) == slot_row
    selector = jnp.where(place, ROW_SCALE, 0.0).astype(jnp.bfloat16)

    lane = lax.broadcasted_iota(jnp.int32, (tokens, LANES), 1)
    holds = lax.rem(lane, slots).astype(jnp.float32) == slot_column
    held = NO_TOKEN + jnp.sum(
        jnp.where(holds, own_column - NO_TOKEN, 0.0), axis=0, keepdims=True
    )
    quotient = jnp.floor(held * (1.0 / RADIX))
    low = lax.broadcasted_iota(jnp.int32, (1, LANES), 1) < slots
    code = jnp.where(low, quotient, held - quotient * RADIX)

    gain = gain_ref[...].astype(jnp.float32)
    copies[2].wait()
    resid = hidden_ref[...].astype(jnp.float32)
    scale = lax.rsqrt(jnp.mean(resid * resid, axis=1, keepdims=True) + 1e-06)
    for block in range(features // LANES):
        lanes = slice(block * LANES, (block + 1) * LANES)
        hidden_ref[:, lanes] = (
            hidden_ref[:, lanes].astype(jnp.float32) * scale * gain[block : block + 1, :]
        ).astype(jnp.bfloat16)
    packed = jnp.dot(selector, hidden_ref[...], preferred_element_type=jnp.float32)
    all_ref[...] = packed.astype(jnp.bfloat16)
    row = lax.broadcasted_iota(jnp.int32, (few, LANES), 0)
    first_ref[:, LANES:] = packed[:few, LANES:].astype(jnp.bfloat16)
    first_ref[:, :LANES] = jnp.where(row == few - 1, code, packed[:few, :LANES]).astype(
        jnp.bfloat16
    )


def pack(hidden, norm_gain, own):
    tokens, features = hidden.shape
    slots = tokens // 2
    few = 3 * slots // 4
    return pl.pallas_call(
        pack_kernel,
        in_specs=[pl.BlockSpec(memory_space=pltpu.HBM)] * 3,
        out_shape=(
            jax.ShapeDtypeStruct((few, features), jnp.bfloat16),
            jax.ShapeDtypeStruct((slots, features), jnp.bfloat16),
            jax.ShapeDtypeStruct((1, tokens), jnp.int32),
            jax.ShapeDtypeStruct((tokens, 1), jnp.float32),
        ),
        scratch_shapes=[
            VMEM((tokens, features), jnp.bfloat16),
            VMEM((features // LANES, LANES), jnp.bfloat16),
            VMEM((1, tokens), jnp.float32),
            pltpu.SemaphoreType.DMA((3,)),
        ],
        compiler_params=pltpu.CompilerParams(vmem_limit_bytes=16 * 1024 * 1024),
    )(hidden, norm_gain.reshape(features // LANES, LANES), own.reshape(1, tokens))


def rank_kernel(devices, cap_rows, rows_ref, asked_ref, scale_ref, weight_ref, many_ref):
    count = rows_ref.shape[0] // devices
    slots = LANES // 2
    lane = lax.broadcasted_iota(jnp.int32, (1, LANES), 1)
    asked = asked_ref[...]
    ahead = jnp.zeros((asked.shape[0], LANES), jnp.float32)
    held = []
    for device in range(devices):
        tile = rows_ref[pl.ds(device * count + count - 16, 16), :LANES].astype(jnp.float32)
        code = tile[15:16, :]
        whole = jnp.where(lane < slots, code * RADIX + pltpu.roll(code, slots, 1), 2.0 * NO_TOKEN)
        held.append(whole)
        ahead += (whole < asked).astype(jnp.float32)
    rank = jnp.sum(ahead, axis=1, keepdims=True)
    weight_ref[...] = jnp.where((asked < NO_TOKEN) & (rank < cap_rows), as_column(scale_ref[...]), 0.0)
    table = jnp.concatenate(held, axis=0)
    last = jnp.sum(
        jnp.where(lax.broadcasted_iota(jnp.int32, table.shape, 1) == count - 1, table, 0.0),
        axis=1,
        keepdims=True,
    )
    ahead = jnp.zeros((devices, LANES), jnp.float32)
    for whole in held:
        ahead += (whole < last).astype(jnp.float32)
    rank = jnp.sum(ahead, axis=1, keepdims=True)
    many = jnp.where((last < NO_TOKEN) & (rank < cap_rows), 1.0, 0.0)
    many_ref[0, 0] = jnp.max(many).astype(jnp.int32)


def ranks(rows, asked, scale, devices, cap_rows):
    return pl.pallas_call(
        functools.partial(rank_kernel, devices, cap_rows),
        in_specs=[pl.BlockSpec(memory_space=VMEM)] * 3,
        out_specs=(
            pl.BlockSpec(memory_space=VMEM),
            pl.BlockSpec(memory_space=pltpu.SMEM),
        ),
        out_shape=(
            jax.ShapeDtypeStruct(asked.shape, jnp.float32),
            jax.ShapeDtypeStruct((1, 1), jnp.int32),
        ),
        compiler_params=pltpu.CompilerParams(vmem_limit_bytes=8 * 1024 * 1024),
    )(rows, asked, scale)


def down_kernel(devices, units_ref, down_ref, share_hbm, spread_ref, hidden_ref, share_ref, sent):
    count = units_ref.shape[1] // devices
    rows = share_ref.shape[0]
    chunk = rows // devices
    copies = []
    ready = 0
    for block, start in enumerate(range(0, rows, ROW_BLOCK)):
        stop = min(rows, start + ROW_BLOCK)
        while ready < devices and ready * chunk < stop:
            slots = pl.ds(ready * count, count)
            gate = units_ref[0, slots, :] * (1.0 / ROW_SCALE)
            up = units_ref[1, slots, :] * (1.0 / ROW_SCALE)
            spread_ref[pl.ds(ready * chunk, count), :] = gate * up / (1.0 + jnp.exp(-gate))
            ready += 1
        hidden_ref[start:stop, :] = spread_ref[start:stop, :].astype(jnp.bfloat16)
        share_ref[start:stop, :] = jnp.dot(
            hidden_ref[start:stop, :], down_ref[...], preferred_element_type=jnp.float32
        ).astype(jnp.bfloat16)
        copy = pltpu.make_async_copy(
            share_ref.at[start:stop, :], share_hbm.at[start:stop, :], sent.at[block]
        )
        copy.start()
        copies.append(copy)
    for copy in copies:
        copy.wait()


def down_share(units, expert_down, devices):
    _, slots, fr_dev = units.shape
    features = expert_down.shape[1]
    chunks = slots - devices
    return pl.pallas_call(
        functools.partial(down_kernel, devices),
        in_specs=[pl.BlockSpec(memory_space=VMEM)] * 2,
        out_specs=pl.BlockSpec(memory_space=pltpu.HBM),
        out_shape=jax.ShapeDtypeStruct((chunks, features), jnp.bfloat16),
        scratch_shapes=[
            VMEM((slots, fr_dev), jnp.float32),
            VMEM((chunks, fr_dev), jnp.bfloat16),
            VMEM((chunks, features), jnp.bfloat16),
            pltpu.SemaphoreType.DMA((pl.cdiv(chunks, ROW_BLOCK),)),
        ],
        compiler_params=pltpu.CompilerParams(vmem_limit_bytes=24 * 1024 * 1024),
        cost_estimate=pl.CostEstimate(
            flops=2 * chunks * fr_dev * features,
            bytes_accessed=2 * fr_dev * features + 2 * chunks * features,
            transcendentals=slots * fr_dev,
        ),
    )(units, expert_down)


def expert_units(rows, expert_gate_up):
    return jnp.einsum("td,dgf->gtf", rows, expert_gate_up, preferred_element_type=jnp.float32)


def wide_share(rows, expert_gate_up, expert_down, chunk):
    devices, count, features = rows.shape
    fr_dev = expert_down.shape[0]
    normed = rows.reshape(devices * count, features).astype(jnp.bfloat16)
    units = expert_units(normed, expert_gate_up) * (1.0 / ROW_SCALE)
    hidden = (jax.nn.silu(units[0]) * units[1]).astype(jnp.bfloat16)
    hidden = jnp.pad(
        hidden.reshape(devices, count, fr_dev), ((0, 0), (0, chunk - count), (0, 0))
    )
    return jnp.dot(
        hidden.reshape(devices * chunk, fr_dev), expert_down, preferred_element_type=jnp.float32
    ).astype(jnp.bfloat16)


def on_device(hidden, norm_gain, route_expert, route_weight, priority, expert_gate_up, expert_down):
    devices = lax.axis_size("sx")
    tok_dev = hidden.shape[0]
    slot_count = tok_dev // 2
    cap_rows = 3 * slot_count * devices // 8
    own = jnp.where(route_expert[:, 0] == 0, priority, NO_TOKEN).astype(jnp.float32)
    first, every, slot, asked = pack(hidden, norm_gain, own)
    gathered = lax.all_gather(first.astype(jnp.float16), "sx", axis=0, tiled=True)
    rows = lax.optimization_barrier(gathered.astype(jnp.bfloat16))
    weight, many = ranks(rows, asked, route_weight.reshape(1, tok_dev), devices, cap_rows)
    rows, weight, crowded = lax.optimization_barrier((rows, weight, many[0, 0] > 0))
    share = down_share(expert_units(rows, expert_gate_up), expert_down, devices)

    def finish(returned):
        place = (
            jnp.arange(returned.shape[0], dtype=jnp.int32)[None, :] == slot.reshape(tok_dev, 1)
        ).astype(jnp.bfloat16)
        routed = jnp.dot(place, returned, preferred_element_type=jnp.float32)
        return (hidden.astype(jnp.float32) + weight * routed).astype(jnp.bfloat16)

    def narrow(share, every):
        return finish(lax.psum_scatter(share, "sx", scatter_dimension=0, tiled=True))

    def wide(share, every):
        rows = lax.all_gather(every.astype(jnp.float16), "sx", axis=0, tiled=False)
        share = wide_share(rows, expert_gate_up, expert_down, slot_count + 15)
        return finish(lax.psum_scatter(share, "sx", scatter_dimension=0, tiled=True))

    return lax.cond(crowded, wide, narrow, share, every)


def solution(mesh):
    in_specs = (
        P(("dp", "sx"), None),
        P(),
        P(("dp", "sx"), None),
        P(("dp", "sx")),
        P(("dp", "sx")),
        P(None, None, "sx"),
        P("sx", None),
    )
    out_specs = P(("dp", "sx"), None)
    return jax.shard_map(
        on_device, mesh=mesh, in_specs=in_specs, out_specs=out_specs, check_vma=False
    )
```

time: 107 us -> 103 us (0.963)
  local copies, waits for them, and re-layouts: 7.19 us -> 3.79 us
  Pallas kernels: 9.43 us -> 8.16 us
    unnamed x19 -> x17, local copies, waits for them, and re-layouts: 6.42 us -> 3.73 us
    pallas_call x2 -> x3, Pallas kernels: 9.43 us -> 8.16 us  [the longest x1 5.53 us: down_share(): pl.pallas_call(functools.partial(down_kernel, devices), in_specs=[pl.Bloc...]
where the time goes in v3:
time: 103 us
  blocking collectives  76.4 us (74%)
  Pallas kernels  8.16 us (8%)
  matrix products  8.07 us (8%)
  local copies, waits for them, and re-layouts  3.79 us (4%)
  starting transfers between devices  1.92 us (2%)
  waiting for transfers between devices  1.78 us (2%)
  other arithmetic  1.47 us (1%)
    all_gather x1, blocking collectives, on_device(): lax.all_gather(first.astype(jnp.float16), 'sx', axis=0, tiled=True)  40 us
    unnamed x1, blocking collectives  36.4 us
    dot_general x1, matrix products, expert_units(): jnp.einsum('td,dgf->gtf', rows, expert_gate_up, preferred_element_type=jn...  6.75 us
    pallas_call x1, Pallas kernels, down_share(): pl.pallas_call(functools.partial(down_kernel, devices), in_specs=[pl.Bloc...  5.53 us
    unnamed x17, local copies, waits for them, and re-layouts  3.73 us
  transfers between devices with their start and end apart: 1, of which 1 were waited for; matrix products, arithmetic and copies ran while one was open for 1% of the time, Pallas kernels for 0%

profile of v3, /device:TPU:1, one launch (start us, length us, event | category | flops | bytes accessed | tf_op | source)
XLA Modules:
  0.0 103.0 jit_solution(17331878439498150725)
XLA Ops:
  0.0 0.7 fusion.27.own_hbm
  0.7 0.0 copy-start
  0.7 0.7 copy-done
  1.4 1.8 %shard_map.75 = (bf16[48,3200]{1,0:T(8,128)(2,1)S(1)}, bf16[64,3200]{1,0:T(8,128)(2,1)S(1)}, s32[1,128]{1,0:T(1,128)S(1)}, f32[128,1]{1,0:T(8,128)S(1)}) custom-call(bf16[128,3200]{1,0:T(8,128)(2,1)} %hidden_hbm.1, bf16[25,128]{1,0:T(8,128)(2,1)S(1)} %bitcast.39, f32[1,128]{1,0:T(1,128)S(1)} %fusion.27.own_hbm), custom_call_target="tpu_custom_call" | custom-call | tf_op jit(solution)/shard_map/pallas_call | solution.py:89
  3.2 0.1 convert_element_type.51
  3.2 0.0 slice-start
  3.2 40.0 %all-gather.4 = f16[768,3200]{1,0:T(8,128)(2,1)S(1)} all-gather(f16[48,3200]{1,0:T(8,128)(2,1)S(1)} %convert_element_type.51), channel_id=1, replica_groups=mesh['dp'=16,'sx'=16] {'sx'}, dimensions={0}, use_global_device_ids=true | all-gather | bytes 5222400 | tf_op jit(solution)/shard_map/all_gather | solution.py:229
  43.2 0.0 copy-start.1
  43.2 0.0 slice-start.1
  43.2 0.7 convert_element_type.52.rows_ref
  43.9 0.0 copy-done.1
  44.0 0.8 shard_map.76
  45.5 0.0 slice-done
  45.5 0.0 slice-done.1
  45.5 0.0 copy-start.3
  45.5 6.7 %fusion.21.units_ref = f32[2,768,640]{2,1,0:T(8,128)S(1)} fusion(bf16[3200,2,640]{2,1,0:T(2,128)(2,1)S(1)} %bitcast.48, bf16[768,3200]{1,0:T(8,128)(2,1)S(1)} %convert_element_type.52.rows_ref), kind=kOutput, calls=%fused_computation.22 | convolution fusion | flops 6291456000 | bytes 17039360 | tf_op jit(solution)/shard_map/td,dgf->gtf/dot_general | solution.py:205
  52.2 0.0 copy-done.3
  52.3 0.0 copy-start.2
  52.3 5.5 %shard_map.77 = bf16[752,3200]{1,0:T(8,128)(2,1)} custom-call(f32[2,768,640]{2,1,0:T(8,128)S(1)} %fusion.21.units_ref, bf16[640,3200]{1,0:T(8,128)(2,1)S(1)} %copy-done.3), custom_call_target="tpu_custom_call" | custom-call | flops 3080192000 | bytes 8908800 | tf_op jit(solution)/shard_map/pallas_call | solution.py:184
  57.8 0.0 copy-done.2
  57.8 45.2 %conditional.7 = (bf16[128,3200]{1,0:T(8,128)(2,1)}) conditional(s32[]{:T(128)} %convert_element_type.53, (bf16[128,3200]{1,0:T(8,128)(2,1)S(1)}, f32[128,1]{1,0:T(8,128)S(1)}, s32[1,128]{1,0:T(1,128)S(1)}, bf16[752,3200]{1,0:T(8,128)(2,1)}) %tuple.39, (bf16[128,3200]{1,0:T(8,128)(2,1)S(1)}, f32[128,1]{1,0:T(8,128)S(1)}, s32[1,128]{1,0:T(1,128)S(1)}, ...), branch_computations={%region_0.2_spmd, %region_2.4_spmd} | conditional | flops 13649182720 | bytes 87815288
  57.8 0.0 copy-start.5
  57.9 36.4 %fusion = bf16[48,3200]{1,0:T(8,128)(2,1)S(1)} fusion(bf16[752,3200]{1,0:T(8,128)(2,1)} %get-tuple-element.37), kind=kCustom, calls=%all-reduce-scatter | all-reduce-scatter fusion | flops 2457601 | bytes 5121024
  94.3 1.9 %collective-permute-start = (bf16[15,3200]{1,0:T(8,128)(2,1)S(1)}, bf16[15,3200]{1,0:T(8,128)(2,1)S(1)}, u32[]{:S(2)}, u32[]{:S(2)}) collective-permute-start(bf16[15,3200]{1,0:T(8,128)(2,1)S(1)} %slice.8), channel_id=1, source_target_pairs={{0,1},{1,2},{2,3},{3,4},{4,5},{5,6},{6,7},{7,8},{8,9},{9,10},{10,1... | collective-permute-start | bytes 288008
  96.2 0.1 copy.23
  96.3 0.0 copy-done.5
  96.3 0.6 dynamic-slice.6
  97.6 1.8 %collective-permute-done = bf16[15,3200]{1,0:T(8,128)(2,1)S(1)} collective-permute-done((bf16[15,3200]{1,0:T(8,128)(2,1)S(1)}, bf16[15,3200]{1,0:T(8,128)(2,1)S(1)}, u32[]{:S(2)}, u32[]{:S(2)}) %collective-permute-start) | collective-permute-done | bytes 96032
  99.3 2.4 %concatenate = bf16[63,3200]{1,0:T(8,128)(2,1)S(1)} concatenate(bf16[15,3200]{1,0:T(8,128)(2,1)S(1)} %collective-permute-done, bf16[48,3200]{1,0:T(8,128)(2,1)S(1)} %fusion), dimensions={0} | concatenate | bytes 806400
  101.7 1.3 %fusion.2 = bf16[128,3200]{1,0:T(8,128)(2,1)} fusion(bf16[128,3200]{1,0:T(8,128)(2,1)S(1)} %get-tuple-element.34, f32[128]{0:T(128)S(1)} %bitcast.43, bf16[63,3200]{1,0:T(8,128)(2,1)S(1)} %concatenate, u32[]{:S(6)} %subtract, s32[128]{0:T(128)S(1)} %bitcast.44), kind=kOutput, calls=%fused_computation.1 | convolution fusion | flops 40146816 | bytes 1946628 | tf_op jit(solution)/shard_map/cond/branch_0_fun/dot_general | solution.py:239
  (2 shorter events, 0.0 us)
Async XLA Ops:
  0.7 0.7 copy-start
  3.2 42.2 %slice-start = ((s8[8192000]{0:T(1024)(128)(4,1)}), s8[4194304]{0:T(1024)(128)(4,1)S(1)}, s32[]{:S(2)}) async-start(s8[8192000]{0:T(1024)(128)(4,1)} %bitcast.47), calls=%async_computation | async-start | bytes 8388608
  43.2 0.7 copy-start.1
  43.2 2.3 %slice-start.1 = ((s8[8192000]{0:T(1024)(128)(4,1)}), s8[3997696]{0:T(1024)(128)(4,1)S(1)}, s32[]{:S(2)}) async-start(s8[8192000]{0:T(1024)(128)(4,1)} %bitcast.47), calls=%async_computation.1 | async-start | bytes 7995392
  45.5 6.8 %copy-start.3 = (bf16[640,3200]{1,0:T(8,128)(2,1)S(1)}, bf16[640,3200]{1,0:T(8,128)(2,1)}, u32[]{:S(2)}) copy-start(bf16[640,3200]{1,0:T(8,128)(2,1)} %down_ref.1) | copy-start | bytes 12288004
  52.3 5.6 %copy-start.2 = (bf16[128,3200]{1,0:T(8,128)(2,1)S(1)}, bf16[128,3200]{1,0:T(8,128)(2,1)}, u32[]{:S(2)}) copy-start(bf16[128,3200]{1,0:T(8,128)(2,1)} %hidden_hbm.1) | copy-start | bytes 2457604
  57.8 38.5 %copy-start.5 = (u32[256]{0:T(256)S(1)}, u32[256]{0:T(256)}, u32[]{:S(2)}) copy-start(u32[256]{0:T(256)} %constant.23) | copy-start | bytes 3076
  94.3 5.0 %collective-permute-start = (bf16[15,3200]{1,0:T(8,128)(2,1)S(1)}, bf16[15,3200]{1,0:T(8,128)(2,1)S(1)}, u32[]{:S(2)}, u32[]{:S(2)}) collective-permute-start(bf16[15,3200]{1,0:T(8,128)(2,1)S(1)} %slice.8), channel_id=1, source_target_pairs={{0,1},{1,2},{2,3},{3,4},{4,5},{5,6},{6,7},{7,8},{8,9},{9,10},{10,1... | collective-permute-start | bytes 288008

commit v4 on v3

--- a/solution.py
+++ b/solution.py
@@ -11,7 +11,9 @@
 NO_TOKEN = 4096
 RADIX = 64
 LANES = 128
-ROW_BLOCK = 256
+COLUMNS = 640
+SPARE = 16
+BLOCKS = (6, 6, 4)
 VMEM = pltpu.VMEM
 
 
@@ -50,7 +52,7 @@
     slot_column = jnp.sum((own < own_column).astype(jnp.float32), axis=1, keepdims=True)
     slot_row = jnp.where(own < NO_TOKEN, slot_row, float(slots))
     slot_column = jnp.where(own_column < NO_TOKEN, slot_column, float(slots))
-    slot_ref[...] = slot_row.astype(jnp.int32)
+    slot_ref[...] = slot_column.astype(jnp.int32)
     asked_ref[...] = own_column
     place = lax.broadcasted_iota(jnp.int32, (slots, tokens), 0).astype(jnp.float32) == slot_row
     selector = jnp.where(place, ROW_SCALE, 0.0).astype(jnp.bfloat16)
@@ -92,7 +94,7 @@
         out_shape=(
             jax.ShapeDtypeStruct((few, features), jnp.bfloat16),
             jax.ShapeDtypeStruct((slots, features), jnp.bfloat16),
-            jax.ShapeDtypeStruct((1, tokens), jnp.int32),
+            jax.ShapeDtypeStruct((tokens, 1), jnp.int32),
             jax.ShapeDtypeStruct((tokens, 1), jnp.float32),
         ),
         scratch_shapes=[
@@ -150,59 +152,102 @@
     )(rows, asked, scale)
 
 
-def down_kernel(devices, units_ref, down_ref, share_hbm, spread_ref, hidden_ref, share_ref, sent):
+def down_kernel(part, units_ref, down_ref, share_hbm, hidden_ref, share_ref, sent):
+    fr_dev, features = down_ref.shape
+    devices = sum(BLOCKS)
     count = units_ref.shape[1] // devices
     rows = share_ref.shape[0]
-    chunk = rows // devices
     copies = []
-    ready = 0
-    for block, start in enumerate(range(0, rows, ROW_BLOCK)):
-        stop = min(rows, start + ROW_BLOCK)
-        while ready < devices and ready * chunk < stop:
-            slots = pl.ds(ready * count, count)
-            gate = units_ref[0, slots, :] * (1.0 / ROW_SCALE)
-            up = units_ref[1, slots, :] * (1.0 / ROW_SCALE)
-            spread_ref[pl.ds(ready * chunk, count), :] = gate * up / (1.0 + jnp.exp(-gate))
-            ready += 1
-        hidden_ref[start:stop, :] = spread_ref[start:stop, :].astype(jnp.bfloat16)
-        share_ref[start:stop, :] = jnp.dot(
-            hidden_ref[start:stop, :], down_ref[...], preferred_element_type=jnp.float32
+    first = 0
+    for block, held in enumerate(BLOCKS):
+        slots = slice(first * count, (first + held) * count)
+        gate = units_ref[0, slots, :] * (1.0 / ROW_SCALE)
+        up = units_ref[1, slots, :] * (1.0 / ROW_SCALE)
+        hidden_ref[slots, :] = (gate * up / (1.0 + jnp.exp(-gate))).astype(jnp.bfloat16)
+        sums = jnp.dot(hidden_ref[slots, :], down_ref[...], preferred_element_type=jnp.float32)
+        for device in range(held):
+            start = (first + device) * part
+            for column in range(features // COLUMNS):
+                share_ref[start : start + count, :] = sums[
+                    device * count : (device + 1) * count,
+                    column * COLUMNS : (column + 1) * COLUMNS,
+                ].astype(jnp.bfloat16)
+                start += count
+            stop = min((first + device + 1) * part, rows)
+            if start < stop:
+                share_ref[start:stop, :] = jnp.zeros((stop - start, COLUMNS), jnp.bfloat16)
+        span = slice(first * part, min((first + held) * part, rows))
+        copy = pltpu.make_async_copy(share_ref.at[span, :], share_hbm.at[span, :], sent.at[block])
+        copy.start()
+        copies.append(copy)
+        first += held
+    for copy in copies:
+        copy.wait()
+
+
+def down_share(units, expert_down, devices):
+    _, slots, fr_dev = units.shape
+    features = expert_down.shape[1]
+    part = features // COLUMNS * (slots // devices) + SPARE
+    rows = devices * (part - 1)
+    return pl.pallas_call(
+        functools.partial(down_kernel, part),
+        in_specs=[pl.BlockSpec(memory_space=VMEM)] * 2,
+        out_specs=pl.BlockSpec(memory_space=pltpu.HBM),
+        out_shape=jax.ShapeDtypeStruct((rows, COLUMNS), jnp.bfloat16),
+        scratch_shapes=[
+            VMEM((slots, fr_dev), jnp.bfloat16),
+            VMEM((rows, COLUMNS), jnp.bfloat16),
+            pltpu.SemaphoreType.DMA((len(BLOCKS),)),
+        ],
+        compiler_params=pltpu.CompilerParams(vmem_limit_bytes=28 * 1024 * 1024),
+        cost_estimate=pl.CostEstimate(
+            flops=2 * slots * fr_dev * features,
+            bytes_accessed=2 * fr_dev * features + 2 * rows * COLUMNS,
+            transcendentals=slots * fr_dev,
+        ),
+    )(units, expert_down)
+
+
+def expert_units(rows, expert_gate_up):
+    return jnp.einsum("td,dgf->gtf", rows, expert_gate_up, preferred_element_type=jnp.float32)
+
+
+def finish_kernel(
+    chunk_ref, slot_ref, weight_ref, hidden_ref, out_hbm, out_ref, sent
+):
+    tokens, features = hidden_ref.shape
+    rows = chunk_ref.shape[0]
+    columns = features // COLUMNS
+    count = (rows + 1 - SPARE) // columns
+    row = lax.broadcasted_iota(jnp.int32, (tokens, rows), 1) - lax.axis_index("sx")
+    copies = []
+    for column in range(columns):
+        lanes = slice(column * COLUMNS, (column + 1) * COLUMNS)
+        place = jnp.where(row == slot_ref[...] + column * count, 1.0, 0.0).astype(jnp.bfloat16)
+        routed = jnp.dot(place, chunk_ref[...], preferred_element_type=jnp.float32)
+        out_ref[:, lanes] = (
+            hidden_ref[:, lanes].astype(jnp.float32) + weight_ref[...] * routed
         ).astype(jnp.bfloat16)
-        copy = pltpu.make_async_copy(
-            share_ref.at[start:stop, :], share_hbm.at[start:stop, :], sent.at[block]
-        )
+        copy = pltpu.make_async_copy(out_ref.at[:, lanes], out_hbm.at[:, lanes], sent.at[column])
         copy.start()
         copies.append(copy)
     for copy in copies:
         copy.wait()
 
 
-def down_share(units, expert_down, devices):
-    _, slots, fr_dev = units.shape
-    features = expert_down.shape[1]
-    chunks = slots - devices
+def finish(chunk, slot, weight, hidden):
     return pl.pallas_call(
-        functools.partial(down_kernel, devices),
-        in_specs=[pl.BlockSpec(memory_space=VMEM)] * 2,
+        finish_kernel,
+        in_specs=[pl.BlockSpec(memory_space=VMEM)] * 4,
         out_specs=pl.BlockSpec(memory_space=pltpu.HBM),
-        out_shape=jax.ShapeDtypeStruct((chunks, features), jnp.bfloat16),
+        out_shape=jax.ShapeDtypeStruct(hidden.shape, hidden.dtype),
         scratch_shapes=[
-            VMEM((slots, fr_dev), jnp.float32),
-            VMEM((chunks, fr_dev), jnp.bfloat16),
-            VMEM((chunks, features), jnp.bfloat16),
-            pltpu.SemaphoreType.DMA((pl.cdiv(chunks, ROW_BLOCK),)),
+            VMEM(hidden.shape, hidden.dtype),
+            pltpu.SemaphoreType.DMA((hidden.shape[1] // COLUMNS,)),
         ],
-        compiler_params=pltpu.CompilerParams(vmem_limit_bytes=24 * 1024 * 1024),
-        cost_estimate=pl.CostEstimate(
-            flops=2 * chunks * fr_dev * features,
-            bytes_accessed=2 * fr_dev * features + 2 * chunks * features,
-            transcendentals=slots * fr_dev,
-        ),
-    )(units, expert_down)
-
-
-def expert_units(rows, expert_gate_up):
-    return jnp.einsum("td,dgf->gtf", rows, expert_gate_up, preferred_element_type=jnp.float32)
+        compiler_params=pltpu.CompilerParams(vmem_limit_bytes=8 * 1024 * 1024),
+    )(chunk, slot, weight, hidden)
 
 
 def wide_share(rows, expert_gate_up, expert_down, chunk):
@@ -232,20 +277,17 @@
     rows, weight, crowded = lax.optimization_barrier((rows, weight, many[0, 0] > 0))
     share = down_share(expert_units(rows, expert_gate_up), expert_down, devices)
 
-    def finish(returned):
-        place = (
-            jnp.arange(returned.shape[0], dtype=jnp.int32)[None, :] == slot.reshape(tok_dev, 1)
-        ).astype(jnp.bfloat16)
-        routed = jnp.dot(place, returned, preferred_element_type=jnp.float32)
-        return (hidden.astype(jnp.float32) + weight * routed).astype(jnp.bfloat16)
-
     def narrow(share, every):
-        return finish(lax.psum_scatter(share, "sx", scatter_dimension=0, tiled=True))
+        chunk = lax.psum_scatter(share, "sx", scatter_dimension=0, tiled=True)
+        return finish(chunk, slot, weight, hidden)
 
     def wide(share, every):
         rows = lax.all_gather(every.astype(jnp.float16), "sx", axis=0, tiled=False)
         share = wide_share(rows, expert_gate_up, expert_down, slot_count + 15)
-        return finish(lax.psum_scatter(share, "sx", scatter_dimension=0, tiled=True))
+        returned = lax.psum_scatter(share, "sx", scatter_dimension=0, tiled=True)
+        place = (jnp.arange(slot_count + 15, dtype=jnp.int32)[None, :] == slot).astype(jnp.bfloat16)
+        routed = jnp.dot(place, returned, preferred_element_type=jnp.float32)
+        return (hidden.astype(jnp.float32) + weight * routed).astype(jnp.bfloat16)
 
     return lax.cond(crowded, wide, narrow, share, every)
 

time: 103 us -> 102 us (level)
  local copies, waits for them, and re-layouts: 3.79 us -> 2.02 us
  matrix products: 8.07 us -> 6.75 us
  Pallas kernels: 8.16 us -> 9.2 us
    cond x0 -> x1, blocking collectives: none -> 36.7 us
    unnamed x1 -> x0, blocking collectives: 36.4 us -> none
    unnamed x17 -> x12, local copies, waits for them, and re-layouts: 3.73 us -> 0.72 us
    unnamed x1 -> x0, starting transfers between devices: 1.92 us -> none
    cond x0 -> x1, starting transfers between devices: none -> 1.92 us
    unnamed x1 -> x0, waiting for transfers between devices: 1.78 us -> none
    cond x0 -> x1, waiting for transfers between devices: none -> 1.7 us
    dot_general x1 -> x0, matrix products: 1.32 us -> none  [finish(): routed = jnp.dot(place, returned, preferred_element_type=jnp.float32)]
where the time goes in v4:
time: 102 us
  blocking collectives  76.7 us (75%)
  Pallas kernels  9.2 us (9%)
  matrix products  6.75 us (7%)
  local copies, waits for them, and re-layouts  2.02 us (2%)
  starting transfers between devices  1.92 us (2%)
  waiting for transfers between devices  1.7 us (2%)
  other arithmetic  1.47 us (1%)
    all_gather x1, blocking collectives, on_device(): lax.all_gather(first.astype(jnp.float16), 'sx', axis=0, tiled=True)  40 us
    cond x1, blocking collectives  36.7 us
    dot_general x1, matrix products, expert_units(): jnp.einsum('td,dgf->gtf', rows, expert_gate_up, preferred_element_type=jn...  6.75 us
    pallas_call x1, Pallas kernels, down_share(): pl.pallas_call(functools.partial(down_kernel, part), in_specs=[pl.BlockSp...  5.33 us
  transfers between devices with their start and end apart: 1, of which 1 were waited for; matrix products, arithmetic and copies ran while one was open for 1% of the time, Pallas kernels for 0%

profile of v4, /device:TPU:1, one launch (start us, length us, event | category | flops | bytes accessed | tf_op | source)
XLA Modules:
  0.0 101.6 jit_solution(13266151197975140389)
XLA Ops:
  0.0 0.7 fusion.24.own_hbm
  0.7 0.0 copy-start
  0.7 0.7 copy-done
  1.4 1.8 %shard_map.75 = (bf16[48,3200]{1,0:T(8,128)(2,1)S(1)}, bf16[64,3200]{1,0:T(8,128)(2,1)S(1)}, s32[128,1]{1,0:T(8,128)S(1)}, f32[128,1]{1,0:T(8,128)S(1)}) custom-call(bf16[128,3200]{1,0:T(8,128)(2,1)} %hidden_hbm.1, bf16[25,128]{1,0:T(8,128)(2,1)S(1)} %bitcast.37, f32[1,128]{1,0:T(1,128)S(1)} %fusion.24.own_hbm), custom_call_target="tpu_custom_call" | custom-call | tf_op jit(solution)/shard_map/pallas_call | solution.py:91
  3.2 0.1 convert_element_type.38
  3.2 0.0 slice-start
  3.2 40.0 %all-gather.4 = f16[768,3200]{1,0:T(8,128)(2,1)S(1)} all-gather(f16[48,3200]{1,0:T(8,128)(2,1)S(1)} %convert_element_type.38), channel_id=1, replica_groups=mesh['dp'=16,'sx'=16] {'sx'}, dimensions={0}, use_global_device_ids=true | all-gather | bytes 5222400 | tf_op jit(solution)/shard_map/all_gather | solution.py:274
  43.2 0.0 copy-start.1
  43.2 0.0 slice-start.1
  43.2 0.7 convert_element_type.39.rows_ref
  43.9 0.0 copy-done.1
  44.0 0.8 shard_map.76
  45.5 0.0 slice-done
  45.5 0.0 slice-done.1
  45.5 0.0 copy-start.3
  45.5 6.7 %fusion.18.units_ref = f32[2,768,640]{2,1,0:T(8,128)S(1)} fusion(bf16[3200,2,640]{2,1,0:T(2,128)(2,1)S(1)} %bitcast.44, bf16[768,3200]{1,0:T(8,128)(2,1)S(1)} %convert_element_type.39.rows_ref), kind=kOutput, calls=%fused_computation.18 | convolution fusion | flops 6291456000 | bytes 17039360 | tf_op jit(solution)/shard_map/td,dgf->gtf/dot_general | solution.py:213
  52.2 0.0 copy-done.3
  52.3 0.0 copy-start.2
  52.3 5.3 %shard_map.77 = bf16[4080,640]{1,0:T(8,128)(2,1)} custom-call(f32[2,768,640]{2,1,0:T(8,128)S(1)} %fusion.18.units_ref, bf16[640,3200]{1,0:T(8,128)(2,1)S(1)} %copy-done.3), custom_call_target="tpu_custom_call" | custom-call | flops 3145728000 | bytes 9318400 | tf_op jit(solution)/shard_map/pallas_call | solution.py:193
  57.6 0.0 copy-done.2
  57.6 43.8 %conditional.1 = (bf16[128,3200]{1,0:T(8,128)(2,1)}) conditional(s32[]{:T(128)} %convert_element_type.40, (bf16[4080,640]{1,0:T(8,128)(2,1)}, s32[128,1]{1,0:T(8,128)S(1)}, f32[128,1]{1,0:T(8,128)S(1)}, bf16[128,3200]{1,0:T(8,128)(2,1)S(1)}) %tuple.23, (bf16[128,3200]{1,0:T(8,128)(2,1)S(1)}, f32[128,1]{1,0:T(8,128)S(1)}, s32[128,1]{1,0:T(8,128)S(1)}, ...), branch_computations={%region_0.2_spmd, %region_2.4_spmd} | conditional | flops 13649182720 | bytes 87820456 | solution.py:292
  57.6 0.0 copy-start.7
  57.6 36.7 %fusion = bf16[256,640]{1,0:T(8,128)(2,1)S(1)} fusion(bf16[4080,640]{1,0:T(8,128)(2,1)} %get-tuple-element.28), kind=kCustom, calls=%all-reduce-scatter | all-reduce-scatter fusion | flops 2621441 | bytes 5551104 | tf_op jit(solution)/shard_map/cond
  94.4 1.9 %collective-permute-start = (bf16[15,640]{1,0:T(8,128)(2,1)S(1)}, bf16[15,640]{1,0:T(8,128)(2,1)S(1)}, u32[]{:S(2)}, u32[]{:S(2)}) collective-permute-start(bf16[15,640]{1,0:T(8,128)(2,1)S(1)} %slice.8), channel_id=1, source_target_pairs={{0,1},{1,2},{2,3},{3,4},{4,5},{5,6},{6,7},{7,8},{8,9},{9,10},{10,1... | collective-permute-start | bytes 57608 | tf_op jit(solution)/shard_map/cond
  96.3 0.0 copy-done.7
  96.3 0.6 dynamic-slice.6
  97.5 1.7 %collective-permute-done = bf16[15,640]{1,0:T(8,128)(2,1)S(1)} collective-permute-done((bf16[15,640]{1,0:T(8,128)(2,1)S(1)}, bf16[15,640]{1,0:T(8,128)(2,1)S(1)}, u32[]{:S(2)}, u32[]{:S(2)}) %collective-permute-start) | collective-permute-done | bytes 19232 | tf_op jit(solution)/shard_map/cond
  99.2 0.6 concatenate
  99.9 0.1 constant_dynamic-slice_fusion.chunk_ref
  100.0 1.2 %branch_0_fun.1 = bf16[128,3200]{1,0:T(8,128)(2,1)} custom-call(bf16[255,640]{1,0:T(8,128)(2,1)S(1)} %constant_dynamic-slice_fusion.chunk_ref, s32[128,1]{1,0:T(8,128)S(1)} %get-tuple-element.29.slot_ref, f32[128,1]{1,0:T(8,128)S(1)} %get-tuple-element.30.weight_ref, bf16[128,3200]{1,0:T(8,128)(2,1)S(1)} %get-tuple-element.31.hidden_ref), custom_call_target="tpu_custom_call" | custom-call | tf_op jit(solution)/shard_map/cond/branch_0_fun/pallas_call | solution.py:240
  (2 shorter events, 0.0 us)
Async XLA Ops:
  0.7 0.7 copy-start
  3.2 42.2 %slice-start = ((s8[8192000]{0:T(1024)(128)(4,1)}), s8[4194304]{0:T(1024)(128)(4,1)S(1)}, s32[]{:S(2)}) async-start(s8[8192000]{0:T(1024)(128)(4,1)} %bitcast.43), calls=%async_computation | async-start | bytes 8388608
  43.2 0.7 copy-start.1
  43.2 2.3 %slice-start.1 = ((s8[8192000]{0:T(1024)(128)(4,1)}), s8[3997696]{0:T(1024)(128)(4,1)S(1)}, s32[]{:S(2)}) async-start(s8[8192000]{0:T(1024)(128)(4,1)} %bitcast.43), calls=%async_computation.1 | async-start | bytes 7995392
  45.5 6.8 %copy-start.3 = (bf16[640,3200]{1,0:T(8,128)(2,1)S(1)}, bf16[640,3200]{1,0:T(8,128)(2,1)}, u32[]{:S(2)}) copy-start(bf16[640,3200]{1,0:T(8,128)(2,1)} %down_ref.1) | copy-start | bytes 12288004
  52.3 5.4 %copy-start.2 = (bf16[128,3200]{1,0:T(8,128)(2,1)S(1)}, bf16[128,3200]{1,0:T(8,128)(2,1)}, u32[]{:S(2)}) copy-start(bf16[128,3200]{1,0:T(8,128)(2,1)} %hidden_hbm.1) | copy-start | bytes 2457604
  57.6 38.7 %copy-start.7 = (u32[256]{0:T(256)S(1)}, u32[256]{0:T(256)}, u32[]{:S(2)}) copy-start(u32[256]{0:T(256)} %constant.23) | copy-start | bytes 3076 | tf_op jit(solution)/shard_map/cond
  94.4 4.9 %collective-permute-start = (bf16[15,640]{1,0:T(8,128)(2,1)S(1)}, bf16[15,640]{1,0:T(8,128)(2,1)S(1)}, u32[]{:S(2)}, u32[]{:S(2)}) collective-permute-start(bf16[15,640]{1,0:T(8,128)(2,1)S(1)} %slice.8), channel_id=1, source_target_pairs={{0,1},{1,2},{2,3},{3,4},{4,5},{5,6},{6,7},{7,8},{8,9},{9,10},{10,1... | collective-permute-start | bytes 57608 | tf_op jit(solution)/shard_map/cond
